TPU v7x, 32 devices: a whole 2x2x4 slice. The times are simulated.
32 devices in a mesh: dp: 2 (over x), fsdp: 16 (over z, y, core).
Axes of the slice: x: 2, y: 2, z: 4, core: 2. Of those that a mesh axis runs over, the one named last changes fastest.
Arguments:
- embeddings: bfloat16 [32768, 512], P(('dp', 'fsdp')), may hold values from -6 to 6
- conv_weight: bfloat16 [2, 2359296], P(None, ('dp', 'fsdp')), may hold values from -0.09375 to 0.09375
- inner_weight: bfloat16 [2, 1048576], P(None, ('dp', 'fsdp')), may hold values from -0.25 to 0.25
- outer_weight: bfloat16 [2, 1048576], P(None, ('dp', 'fsdp')), may hold values from -0.125 to 0.125
- vectors: bfloat16 [2, 3584], P(None, ('dp', 'fsdp')), may hold values from -2 to 3
- cotangent: bfloat16 [32768, 512], P(('dp', 'fsdp')), may hold values from -6 to 6
- row_mask: int32 [32768], P(('dp', 'fsdp')), may hold values 0 or 1
Outputs:
- output: bfloat16 [32768, 512], P(('dp', 'fsdp'))
- grad_embeddings: bfloat16 [32768, 512], P(('dp', 'fsdp'))
- grad_conv: float32 [2, 2359296], P(None, ('dp', 'fsdp'))
- grad_inner: float32 [2, 1048576], P(None, ('dp', 'fsdp'))
- grad_outer: float32 [2, 1048576], P(None, ('dp', 'fsdp'))
- grad_vectors: float32 [2, 3584], P(None, ('dp', 'fsdp'))
All inputs are finite; a program needn't handle non-finite values. No bound on the sum of `row_mask` on one device may be relied on, other than what follows from the above.
Results may differ from a plain program's by a relative error of at most 0.013.
Values may be sent and summed in bfloat16 or wider, within the bound.
A program may use at most 192 MiB of HBM per device.

v0:
```python
import jax
import jax.numpy as jnp
from jax import lax
from jax.sharding import PartitionSpec as P

D = 512
FF = 2048
KS = 9
L = 512
MICRO = 2


def shortened(x):
    return jax.tree.map(lambda a: a.astype(jnp.bfloat16) if a.dtype == jnp.float32 else a, x)


def normalize(values):
    centered = values - jnp.mean(values, axis=-1, keepdims=True)
    return centered * lax.rsqrt(jnp.mean(centered * centered, axis=-1, keepdims=True) + 1e-05)


def conv_branch(values):
    return normalize(jax.nn.gelu(values))


def contract_rows(left, right):
    return lax.dot_general(
        left, right, (((0,), (0,)), ((), ())), preferred_element_type=jnp.float32
    )


def contract_cols(left, right):
    return lax.dot_general(
        left, right, (((1,), (1,)), ((), ())), preferred_element_type=jnp.float32
    )


def unpack(members):
    conv_flat, inner_flat, outer_flat, vector_flat = members
    return (
        conv_flat.reshape(KS * D, D),
        inner_flat.reshape(D, FF),
        outer_flat.reshape(FF, D),
        vector_flat.astype(jnp.float32),
    )


def columns(stream_low, dilation):
    windows = stream_low.shape[0] // L
    framed = stream_low.reshape(windows, L, D)
    margin = KS // 2 * dilation
    padded = jnp.pad(framed, ((0, 0), (margin, margin), (0, 0)))
    stacked = jnp.stack(
        [padded[:, tap_id * dilation : tap_id * dilation + L] for tap_id in range(KS)], axis=2
    )
    return stacked.reshape(windows * L, KS * D)


def fold_back(grad_cols, dilation):
    windows = grad_cols.shape[0] // L
    framed = grad_cols.reshape(windows, L, KS, D)
    margin = KS // 2 * dilation
    total = jnp.zeros((windows, L + 2 * margin, D), jnp.float32)
    for tap_id in range(KS):
        before = tap_id * dilation
        total = total + jnp.pad(
            framed[:, :, tap_id], ((0, 0), (before, 2 * margin - before), (0, 0))
        )
    return total[:, margin : margin + L].reshape(windows * L, D)


def block_forward(stream, weights, dilation):
    conv_mat, inner_mat, outer_mat, vector = weights
    conv_bias = vector[:D]
    gain_conv = vector[D : 2 * D]
    gain_ffn = vector[2 * D : 3 * D]
    bias_ffn = vector[3 * D :]
    stream_low = stream.astype(jnp.bfloat16)
    pre_conv = (
        jnp.dot(columns(stream_low, dilation), conv_mat, preferred_element_type=jnp.float32)
        + conv_bias
    )
    mixed = stream + gain_conv * conv_branch(pre_conv)
    mixed_low = mixed.astype(jnp.bfloat16)
    pre_ffn = jnp.dot(mixed_low, inner_mat, preferred_element_type=jnp.float32) + bias_ffn
    hidden_low = jax.nn.gelu(pre_ffn).astype(jnp.bfloat16)
    branch = jnp.dot(hidden_low, outer_mat, preferred_element_type=jnp.float32)
    result = mixed + gain_ffn * normalize(branch)
    return (result, (stream_low, pre_conv, mixed_low, pre_ffn, hidden_low, branch))


def block_backward(grad_out, saved, weights, dilation):
    conv_mat, inner_mat, outer_mat, vector = weights
    gain_conv = vector[D : 2 * D]
    gain_ffn = vector[2 * D : 3 * D]
    stream_low, pre_conv, mixed_low, pre_ffn, hidden_low, branch = saved
    normed_branch, branch_back = jax.vjp(normalize, branch)
    grad_gain_ffn = jnp.sum(grad_out * normed_branch, axis=0)
    grad_branch = branch_back(grad_out * gain_ffn)[0].astype(jnp.bfloat16)
    grad_outer = contract_rows(hidden_low, grad_branch)
    grad_hidden = contract_cols(grad_branch, outer_mat)
    _, gelu_back = jax.vjp(jax.nn.gelu, pre_ffn)
    grad_pre_ffn = gelu_back(grad_hidden)[0].astype(jnp.bfloat16)
    grad_bias_ffn = jnp.sum(grad_pre_ffn.astype(jnp.float32), axis=0)
    grad_inner = contract_rows(mixed_low, grad_pre_ffn)
    grad_mixed = grad_out + contract_cols(grad_pre_ffn, inner_mat)
    normed_conv, conv_back = jax.vjp(conv_branch, pre_conv)
    grad_gain_conv = jnp.sum(grad_mixed * normed_conv, axis=0)
    grad_pre_conv = conv_back(grad_mixed * gain_conv)[0].astype(jnp.bfloat16)
    grad_conv_bias = jnp.sum(grad_pre_conv.astype(jnp.float32), axis=0)
    grad_kernel = contract_rows(columns(stream_low, dilation), grad_pre_conv)
    grad_stream = grad_mixed + fold_back(contract_cols(grad_pre_conv, conv_mat), dilation)
    weight_grads = (
        grad_kernel.reshape(-1),
        grad_inner.reshape(-1),
        grad_outer.reshape(-1),
        jnp.concatenate([grad_conv_bias, grad_gain_conv, grad_gain_ffn, grad_bias_ffn]),
    )
    return (grad_stream, weight_grads)


def reduce_both(members):
    count_dp = lax.axis_size("dp")
    count_fsdp = lax.axis_size("fsdp")
    shaped = tuple(
        (
            member.reshape(2, count_dp, count_fsdp, member.shape[1] // (count_dp * count_fsdp))
            for member in members
        )
    )
    spread = jax.tree.map(
        lambda part, own: part.astype(own.dtype),
        lax.all_to_all(shortened(shaped), "fsdp", split_axis=2, concat_axis=2, tiled=True),
        shaped,
    )
    partial_sums = tuple((jnp.sum(member, axis=2, keepdims=True) for member in spread))
    settled = jax.tree.map(
        lambda part, own: part.astype(own.dtype),
        lax.all_to_all(shortened(partial_sums), "dp", split_axis=1, concat_axis=1, tiled=True),
        partial_sums,
    )
    return tuple((jnp.sum(member, axis=(1, 2)) for member in settled))


def body(embeddings, conv_weight, inner_weight, outer_weight, vectors, cotangent, row_mask):
    spread_taps = (2, 16)
    rows_micro = embeddings.shape[0] // MICRO
    outputs = []
    input_grads = []
    totals = [None, None]
    for micro_id in range(MICRO):
        offset = micro_id * rows_micro
        stream = embeddings[offset : offset + rows_micro].astype(jnp.float32)
        saved_list = []
        for block_id in range(2):
            stream, saved = block_forward(
                stream,
                unpack(
                    (
                        lax.all_gather(conv_weight[block_id], ("dp", "fsdp"), axis=0, tiled=True),
                        lax.all_gather(inner_weight[block_id], ("dp", "fsdp"), axis=0, tiled=True),
                        lax.all_gather(outer_weight[block_id], ("dp", "fsdp"), axis=0, tiled=True),
                        lax.all_gather(vectors[block_id], ("dp", "fsdp"), axis=0, tiled=True),
                    )
                ),
                spread_taps[block_id],
            )
            saved_list.append(saved)
        outputs.append(stream.astype(jnp.bfloat16))
        mask_rows = row_mask[offset : offset + rows_micro].astype(jnp.float32)[:, None]
        grad_stream = cotangent[offset : offset + rows_micro].astype(jnp.float32) * mask_rows
        for block_id in (1, 0):
            grad_stream, weight_grads = block_backward(
                grad_stream,
                saved_list[block_id],
                unpack(
                    (
                        lax.all_gather(conv_weight[block_id], ("dp", "fsdp"), axis=0, tiled=True),
                        lax.all_gather(inner_weight[block_id], ("dp", "fsdp"), axis=0, tiled=True),
                        lax.all_gather(outer_weight[block_id], ("dp", "fsdp"), axis=0, tiled=True),
                        lax.all_gather(vectors[block_id], ("dp", "fsdp"), axis=0, tiled=True),
                    )
                ),
                spread_taps[block_id],
            )
            if totals[block_id] is None:
                totals[block_id] = weight_grads
            else:
                totals[block_id] = tuple(
                    (total + update for total, update in zip(totals[block_id], weight_grads))
                )
        input_grads.append(grad_stream.astype(jnp.bfloat16))
    stacked = tuple(
        (jnp.stack([totals[0][member_id], totals[1][member_id]]) for member_id in range(4))
    )
    summed = reduce_both(stacked)
    output = jnp.concatenate(outputs, axis=0)
    grad_embeddings = jnp.concatenate(input_grads, axis=0)
    return (output, grad_embeddings, summed[0], summed[1], summed[2], summed[3])


def solution(mesh):
    in_specs = (
        P(("dp", "fsdp"), None),
        P(None, ("dp", "fsdp")),
        P(None, ("dp", "fsdp")),
        P(None, ("dp", "fsdp")),
        P(None, ("dp", "fsdp")),
        P(("dp", "fsdp"), None),
        P(("dp", "fsdp")),
    )
    out_specs = (
        P(("dp", "fsdp"), None),
        P(("dp", "fsdp"), None),
        P(None, ("dp", "fsdp")),
        P(None, ("dp", "fsdp")),
        P(None, ("dp", "fsdp")),
        P(None, ("dp", "fsdp")),
    )
    return jax.shard_map(body, mesh=mesh, in_specs=in_specs, out_specs=out_specs, check_vma=False)
```

profile of v0, /device:TPU:12, one launch (start us, length us, event | category | flops | bytes accessed | tf_op | source)
XLA Modules:
  0.0 1209.4 jit_solution(17230627849418039590)
XLA Ops:
  16.7 42.2 %all-reduce.42 = (bf16[3584]{0:T(1024)(128)(2,1)S(1)}, bf16[3584]{0:T(1024)(128)(2,1)S(1)}) all-reduce(bf16[3584]{0:T(1024)(128)(2,1)S(1)} %dynamic-update-slice, bf16[3584]{0:T(1024)(128)(2,1)S(1)} %dynamic-update-slice.1), channel_id=2, replica_groups=mesh['dp'=2,'fsdp'=16] {'dp','fsdp'}, use_global_device_ids=true, to_apply=%add.40 | all-reduce | flops 7168 | bytes 28672
  69.8 5.0 all-gather.23.cloned.1.call-done
  74.8 44.5 %reduce.8 = bf16[1048576]{0:T(1024)(128)(2,1)S(1)} reduce(bf16[1,1048576]{1,0:T(2,128)(2,1)} %all-gather.23.cloned.1.call-done, bf16[]{:T(256)} %constant.161), dimensions={0}, to_apply=%all-gather.6.reduce_sub_computation | reduce | bytes 4194306 | tf_op jit(solution)/shard_map/all_gather | solution.py:161
  121.6 17.3 %all-gather.17.cloned.1.call-done = bf16[1,1048576]{1,0:T(2,128)(2,1)} async-done(((bf16[1,32768]{1,0:T(2,128)(2,1)}), bf16[1,1048576]{1,0:T(2,128)(2,1)}) %all-gather.17.cloned.1.call-update) | async-done | bytes 2097168 | tf_op jit(solution)/shard_map/all_gather | solution.py:161
  138.9 44.9 %reduce.5 = bf16[1048576]{0:T(1024)(128)(2,1)S(1)} reduce(bf16[1,1048576]{1,0:T(2,128)(2,1)} %all-gather.17.cloned.1.call-done, bf16[]{:T(256)} %constant.161), dimensions={0}, to_apply=%all-gather.2.reduce_sub_computation | reduce | bytes 4194306 | tf_op jit(solution)/shard_map/all_gather | solution.py:161
  186.1 16.4 %all-gather.25.cloned.1.call-done = bf16[1,1048576]{1,0:T(2,128)(2,1)} async-done(((bf16[1,32768]{1,0:T(2,128)(2,1)}), bf16[1,1048576]{1,0:T(2,128)(2,1)}) %all-gather.25.cloned.1.call-update) | async-done | bytes 2097168 | tf_op jit(solution)/shard_map/all_gather | solution.py:162
  202.4 44.5 %reduce.9 = bf16[1048576]{0:T(1024)(128)(2,1)S(1)} reduce(bf16[1,1048576]{1,0:T(2,128)(2,1)} %all-gather.25.cloned.1.call-done, bf16[]{:T(256)} %constant.161), dimensions={0}, to_apply=%all-gather.7.reduce_sub_computation | reduce | bytes 4194306 | tf_op jit(solution)/shard_map/all_gather | solution.py:162
  249.5 16.3 %all-gather.19.cloned.1.call-done = bf16[1,1048576]{1,0:T(2,128)(2,1)} async-done(((bf16[1,32768]{1,0:T(2,128)(2,1)}), bf16[1,1048576]{1,0:T(2,128)(2,1)}) %all-gather.19.cloned.1.call-update) | async-done | bytes 2097168 | tf_op jit(solution)/shard_map/all_gather | solution.py:162
  265.8 44.7 %reduce.6 = bf16[1048576]{0:T(1024)(128)(2,1)S(1)} reduce(bf16[1,1048576]{1,0:T(2,128)(2,1)} %all-gather.19.cloned.1.call-done, bf16[]{:T(256)} %constant.161), dimensions={0}, to_apply=%all-gather.3.reduce_sub_computation | reduce | bytes 4194306 | tf_op jit(solution)/shard_map/all_gather | solution.py:162
  313.1 36.8 %all-gather.21.cloned.1.call-done = bf16[1,2359296]{1,0:T(2,128)(2,1)} async-done(((bf16[1,73728]{1,0:T(2,128)(2,1)}), bf16[1,2359296]{1,0:T(2,128)(2,1)}) %all-gather.21.cloned.1.call-update) | async-done | bytes 4718608 | tf_op jit(solution)/shard_map/all_gather | solution.py:160
  349.9 101.1 %reduce.7 = bf16[2359296]{0:T(1024)(128)(2,1)} reduce(bf16[1,2359296]{1,0:T(2,128)(2,1)} %all-gather.21.cloned.1.call-done, bf16[]{:T(256)} %constant.161), dimensions={0}, to_apply=%all-gather.5.reduce_sub_computation | reduce | bytes 9437186 | tf_op jit(solution)/shard_map/all_gather | solution.py:160
  451.0 8.5 dot_general.134
  459.5 8.9 reshape.573
  468.4 101.1 %reduce.4 = bf16[2359296]{0:T(1024)(128)(2,1)} reduce(bf16[1,2359296]{1,0:T(2,128)(2,1)} %all-gather.15.cloned.1.call-done, bf16[]{:T(256)} %constant.161), dimensions={0}, to_apply=%all-gather.1.reduce_sub_computation | reduce | bytes 9437186 | tf_op jit(solution)/shard_map/all_gather | solution.py:160
  569.6 8.5 reshape.568
  578.1 6.4 fusion.176
  584.9 6.1 fusion.171
  593.0 5.7 multiply_convert_fusion.3
  627.4 4.4 convert_reduce_fusion
  635.0 4.5 convert_reduce_fusion.1
  649.1 4.8 convolution_bitcast_fusion.1
  660.1 4.4 multiply_reduce_fusion.4
  702.4 5.2 all-to-all-start.6
  707.6 5.9 add_convert_fusion.5
  720.4 5.0 copy.100
  727.8 5.2 copy.99
  737.0 9.6 pad_maximum_fusion.1
  746.6 6.5 all-to-all-start.2
  775.7 7.9 pad_maximum_fusion.2
  783.6 61.7 %all-to-all-done.2 = bf16[2,2,16,32768]{3,1,0,2:T(2,128)(2,1)} async-done(((bf16[2,2,16,32768]{3,1,0,2:T(2,128)(2,1)}), bf16[2,2,16,32768]{3,1,0,2:T(2,128)(2,1)}, u32[]{:S(2)}, u32[]{:S(2)}) %all-to-all-start.2) | async-done | bytes 4194336 | tf_op jit(solution)/shard_map/all_to_all | solution.py:133
  845.3 5.8 all-to-all-start.4
  851.1 4.7 fusion.200
  860.1 6.1 add.639
  866.2 9.5 copy.97
  875.7 4.7 fusion.199
  880.4 4.3 add_convert_fusion.1
  884.8 6.2 add.637
  891.0 9.3 copy.96
  900.3 6.3 reduce_sum.569
  907.6 35.7 %all-to-all-done.4 = bf16[2,2,16,32768]{3,1,0,2:T(2,128)(2,1)} async-done(((bf16[2,2,16,32768]{3,1,0,2:T(2,128)(2,1)}), bf16[2,2,16,32768]{3,1,0,2:T(2,128)(2,1)}, u32[]{:S(2)}, u32[]{:S(2)}) %all-to-all-start.4) | async-done | bytes 4194336 | tf_op jit(solution)/shard_map/all_to_all | solution.py:133
  946.7 15.0 %pad_maximum_fusion = bf16[2,2,16,73728]{3,1,0,2:T(2,128)(2,1)} fusion(bf16[1,2,16,73728]{3,1,0,2:T(2,128)(2,1)} %copy.97, bf16[1,2,16,73728]{3,1,0,2:T(2,128)(2,1)} %copy.96), kind=kLoop, calls=%fused_computation | loop fusion | flops 4718592 | bytes 18874368 | tf_op jit(solution)/shard_map/stack | solution.py:194
  961.7 5.0 all-to-all-start
  966.8 8.6 dot_general.139
  976.9 4.9 convolution_bitcast_fusion
  1000.9 6.6 reduce_sum.574
  1008.4 163.0 %all-to-all-done = bf16[2,2,16,73728]{3,1,0,2:T(2,128)(2,1)} async-done(((bf16[2,2,16,73728]{3,1,0,2:T(2,128)(2,1)}), bf16[2,2,16,73728]{3,1,0,2:T(2,128)(2,1)}, u32[]{:S(2)}, u32[]{:S(2)}) %all-to-all-start) | async-done | bytes 9437216 | tf_op jit(solution)/shard_map/all_to_all | solution.py:133
  1176.4 9.7 reduce_sum.567
  1193.6 7.1 all-to-all-done.1
  (359 shorter events, 196.8 us)
Async XLA Ops:
  7.2 51.8 %copy-start.70 = (bf16[1024,512]{1,0:T(8,128)(2,1)S(1)}, bf16[1024,512]{1,0:T(8,128)(2,1)}, u32[]{:S(2)}) copy-start(bf16[1024,512]{1,0:T(8,128)(2,1)} %param.7) | copy-start | bytes 3145732
  7.2 67.6 %all-gather.23.cloned.1.call-start = ((), (), s32[]{:S(2)}) async-start(), calls=%async_computation.12 | async-start | bytes 4325376 | tf_op jit(solution)/shard_map/all_gather | solution.py:161
  9.2 129.7 %all-gather.17.cloned.1.call-start = ((), (), s32[]{:S(2)}) async-start(), calls=%async_computation.9 | async-start | bytes 4325376 | tf_op jit(solution)/shard_map/all_gather | solution.py:161
  10.0 192.4 %all-gather.25.cloned.1.call-start = ((), (), s32[]{:S(2)}) async-start(), calls=%async_computation.13 | async-start | bytes 4325376 | tf_op jit(solution)/shard_map/all_gather | solution.py:162
  11.9 253.9 %all-gather.19.cloned.1.call-start = ((), (), s32[]{:S(2)}) async-start(), calls=%async_computation.10 | async-start | bytes 4325376 | tf_op jit(solution)/shard_map/all_gather | solution.py:162
  12.5 337.4 %all-gather.21.cloned.1.call-start = ((), (), s32[]{:S(2)}) async-start(), calls=%async_computation.11 | async-start | bytes 9732096 | tf_op jit(solution)/shard_map/all_gather | solution.py:160
  15.0 453.5 %all-gather.15.cloned.1.call-start = ((), (), s32[]{:S(2)}) async-start(), calls=%async_computation.8 | async-start | bytes 9732096 | tf_op jit(solution)/shard_map/all_gather | solution.py:160
  65.4 4.4 copy-start.71
  578.0 6.8 copy-start.31
  584.9 6.5 copy-start.17
  591.0 11.3 copy-start.5
  593.0 5.7 copy-start.46
  593.0 5.7 copy-start.61
  623.0 12.0 copy-start.15
  625.0 6.9 copy-start.13
  635.0 10.8 copy-start.51
  657.0 7.5 slice-start
  660.1 4.4 copy-start.32
  677.5 7.0 copy-start.49
  677.5 8.7 copy-start.53
  686.2 12.3 %copy-start.48 = (f32[512,512]{0,1:T(8,128)}, f32[512,512]{0,1:T(8,128)S(1)}, u32[]{:S(2)}) copy-start(f32[512,512]{0,1:T(8,128)S(1)} %get-tuple-element.172) | copy-start | bytes 3145732
  702.4 30.6 %all-to-all-start.6 = ((bf16[2,2,16,112]{3,1,0,2:T(2,128)(2,1)}), bf16[2,2,16,112]{3,1,0,2:T(2,128)(2,1)S(1)}, u32[]{:S(2)}, u32[]{:S(2)}) async-start(bf16[2,2,16,112]{3,1,0,2:T(2,128)(2,1)} %copy.105), calls=%async_computation.6 | async-start | bytes 32768 | tf_op jit(solution)/shard_map/all_to_all | solution.py:133
  707.6 5.9 copy-start
  707.6 5.9 copy-start.68
  716.1 9.4 copy-start.20
  727.8 9.2 copy-start.21
  733.6 13.0 %all-to-all-start.7 = ((bf16[2,2,1,112]{3,0,2,1:T(2,128)(2,1)}), bf16[2,2,1,112]{3,0,2,1:T(2,128)(2,1)S(1)}, u32[]{:S(2)}, u32[]{:S(2)}) async-start(bf16[2,2,1,112]{3,0,2,1:T(2,128)(2,1)} %copy.106), calls=%async_computation.7 | async-start | bytes 2048 | tf_op jit(solution)/shard_map/all_to_all | solution.py:139
  746.6 6.5 copy-start.16
  746.6 6.5 copy-start.26
  746.6 98.7 %all-to-all-start.2 = ((bf16[2,2,16,32768]{3,1,0,2:T(2,128)(2,1)}), bf16[2,2,16,32768]{3,1,0,2:T(2,128)(2,1)}, u32[]{:S(2)}, u32[]{:S(2)}) async-start(bf16[2,2,16,32768]{3,1,0,2:T(2,128)(2,1)} %pad_maximum_fusion.1), calls=%async_computation.2 | async-start | bytes 8388608 | tf_op jit(solution)/shard_map/all_to_all | solution.py:133
  759.4 6.5 copy-start.54
  783.6 67.5 %copy-start.33 = (bf16[512,512]{0,1:T(8,128)(2,1)S(1)}, bf16[512,512]{0,1:T(8,128)(2,1)}, u32[]{:S(2)}) copy-start(bf16[512,512]{0,1:T(8,128)(2,1)} %get-tuple-element.61) | copy-start | bytes 1572868
  845.3 10.5 slice-start.4
  845.3 98.0 %all-to-all-start.4 = ((bf16[2,2,16,32768]{3,1,0,2:T(2,128)(2,1)}), bf16[2,2,16,32768]{3,1,0,2:T(2,128)(2,1)}, u32[]{:S(2)}, u32[]{:S(2)}) async-start(bf16[2,2,16,32768]{3,1,0,2:T(2,128)(2,1)} %pad_maximum_fusion.2), calls=%async_computation.4 | async-start | bytes 8388608 | tf_op jit(solution)/shard_map/all_to_all | solution.py:133
  851.1 4.7 slice-start.5
  851.1 4.7 copy-start.29
  866.2 9.5 copy-start.34
  866.2 14.2 %slice-start.6 = ((s8[4718592]{0:T(1024)(128)(4,1)}), s8[524288]{0:T(1024)(128)(4,1)S(1)}, s32[]{:S(2)}) async-start(s8[4718592]{0:T(1024)(128)(4,1)} %bitcast.369), calls=%async_computation.20 | async-start | bytes 1048576
  875.7 4.7 slice-start.7
  875.7 4.7 copy-start.30
  943.2 18.5 %all-to-all-start.3 = ((bf16[2,2,1,32768]{3,0,2,1:T(2,128)(2,1)}), bf16[2,2,1,32768]{3,0,2,1:T(2,128)(2,1)S(1)}, u32[]{:S(2)}, u32[]{:S(2)}) async-start(bf16[2,2,1,32768]{3,0,2,1:T(2,128)(2,1)} %copy.101), calls=%async_computation.3 | async-start | bytes 524288 | tf_op jit(solution)/shard_map/all_to_all | solution.py:139
  961.7 209.7 %all-to-all-start = ((bf16[2,2,16,73728]{3,1,0,2:T(2,128)(2,1)}), bf16[2,2,16,73728]{3,1,0,2:T(2,128)(2,1)}, u32[]{:S(2)}, u32[]{:S(2)}) async-start(bf16[2,2,16,73728]{3,1,0,2:T(2,128)(2,1)} %pad_maximum_fusion), calls=%async_computation | async-start | bytes 18874368 | tf_op jit(solution)/shard_map/all_to_all | solution.py:133
  966.8 8.6 copy-start.64
  966.8 8.6 copy-start.69
  976.9 10.6 slice-start.2
  981.8 5.7 slice-start.3
  1171.5 16.0 %all-to-all-start.5 = ((bf16[2,2,1,32768]{3,0,2,1:T(2,128)(2,1)}), bf16[2,2,1,32768]{3,0,2,1:T(2,128)(2,1)S(1)}, u32[]{:S(2)}, u32[]{:S(2)}) async-start(bf16[2,2,1,32768]{3,0,2,1:T(2,128)(2,1)} %copy.104), calls=%async_computation.5 | async-start | bytes 524288 | tf_op jit(solution)/shard_map/all_to_all | solution.py:139
  1187.5 13.2 %all-to-all-start.1 = ((bf16[2,2,1,73728]{3,0,2,1:T(2,128)(2,1)}), bf16[2,2,1,73728]{3,0,2,1:T(2,128)(2,1)S(1)}, u32[]{:S(2)}, u32[]{:S(2)}) async-start(bf16[2,2,1,73728]{3,0,2,1:T(2,128)(2,1)} %copy.98), calls=%async_computation.1 | async-start | bytes 1179648 | tf_op jit(solution)/shard_map/all_to_all | solution.py:139
  (49 other events, 139.2 us)
Sparse Core Ops, SparseCore 0:
  11.5 63.2 all-gather.22
  78.2 60.6 all-gather.16
  141.8 60.6 all-gather.24
  205.2 60.6 all-gather.18
  269.1 80.7 all-gather.20
  353.3 80.6 all-gather.14
where the time goes:
time: 1220 us; the launch traced here: 1210 us
  other arithmetic  481 us (39%)
  waiting for transfers between devices  361 us (30%)
  local copies, waits for them, and re-layouts  155 us (13%)
  matrix products  118 us (10%)
  blocking collectives  42.2 us (3%)
  starting transfers between devices  36.5 us (3%)
  between operations  16.3 us (1%)
    all_to_all x4, waiting for transfers between devices, reduce_both(): lax.all_to_all(shortened(shaped), 'fsdp', split_axis=2, concat_axis=2, ti...  260 us
    all_gather x2, other arithmetic, body(): lax.all_gather(conv_weight[block_id], ('dp', 'fsdp'), axis=0, tiled=True)  202 us
    all_gather x2, other arithmetic, body(): lax.all_gather(inner_weight[block_id], ('dp', 'fsdp'), axis=0, tiled=True)  89.4 us
    all_gather x2, other arithmetic, body(): lax.all_gather(outer_weight[block_id], ('dp', 'fsdp'), axis=0, tiled=True)  89.2 us
    add x14, local copies, waits for them, and re-layouts, body(): total + update  61.2 us
    dot_general x12, matrix products, contract_rows(): lax.dot_general(left, right, (((0,), (0,)), ((), ())), preferred_element_...  42.2 us
    unnamed x1, blocking collectives  42.2 us
    dot_general x12, matrix products, contract_cols(): lax.dot_general(left, right, (((1,), (1,)), ((), ())), preferred_element_...  39.3 us
  transfers between devices with their start and end apart: 14, of which 9 were waited for; matrix products, arithmetic and copies ran while one was open for 42% of the time, Pallas kernels for 0%

commit v1 on v0

v1 whole, which is shorter than its diff:
```python
import functools

import jax
import jax.numpy as jnp
from jax import lax
from jax.experimental import pallas as pl
from jax.experimental.pallas import tpu as pltpu
from jax.sharding import PartitionSpec as P

D = 512
FF = 2048
KS = 9
L = 512
NV = 3 * D + FF
DILATIONS = (2, 16)
MESH = pl.DeviceIdType.MESH
BF = jnp.bfloat16
F32 = jnp.float32
NX, NZ, NY = 2, 4, 2
NDEV = 32


def normalize(values):
    centered = values - jnp.mean(values, axis=-1, keepdims=True)
    return centered * lax.rsqrt(jnp.mean(centered * centered, axis=-1, keepdims=True) + 1e-05)


def conv_branch(values):
    return normalize(jax.nn.gelu(values))


def contract_rows(left, right):
    return lax.dot_general(left, right, (((0,), (0,)), ((), ())), preferred_element_type=F32)


def contract_cols(left, right):
    return lax.dot_general(left, right, (((1,), (1,)), ((), ())), preferred_element_type=F32)


def columns(stream_low, dilation):
    windows = stream_low.shape[0] // L
    framed = stream_low.reshape(windows, L, D)
    margin = KS // 2 * dilation
    padded = jnp.pad(framed, ((0, 0), (margin, margin), (0, 0)))
    stacked = jnp.concatenate(
        [padded[:, tap_id * dilation : tap_id * dilation + L] for tap_id in range(KS)], axis=2
    )
    return stacked.reshape(windows * L, KS * D)


def fold_back(grad_cols, dilation):
    windows = grad_cols.shape[0] // L
    framed = grad_cols.reshape(windows, L, KS, D)
    margin = KS // 2 * dilation
    total = jnp.zeros((windows, L + 2 * margin, D), F32)
    for tap_id in range(KS):
        before = tap_id * dilation
        total = total + jnp.pad(
            framed[:, :, tap_id], ((0, 0), (before, 2 * margin - before), (0, 0))
        )
    return total[:, margin : margin + L].reshape(windows * L, D)


def block_forward(stream, weights, dilation):
    conv_mat, inner_mat, outer_mat, vector = weights
    conv_bias = vector[:D]
    gain_conv = vector[D : 2 * D]
    gain_ffn = vector[2 * D : 3 * D]
    bias_ffn = vector[3 * D :]
    stream_low = stream.astype(BF)
    pre_conv = (
        jnp.dot(columns(stream_low, dilation), conv_mat, preferred_element_type=F32) + conv_bias
    )
    mixed = stream + gain_conv * conv_branch(pre_conv)
    mixed_low = mixed.astype(BF)
    pre_ffn = jnp.dot(mixed_low, inner_mat, preferred_element_type=F32) + bias_ffn
    hidden_low = jax.nn.gelu(pre_ffn).astype(BF)
    branch = jnp.dot(hidden_low, outer_mat, preferred_element_type=F32)
    result = mixed + gain_ffn * normalize(branch)
    return (result, (stream_low, pre_conv, mixed_low, pre_ffn, hidden_low, branch))


def block_backward(grad_out, saved, weights, dilation):
    conv_mat, inner_mat, outer_mat, vector = weights
    gain_conv = vector[D : 2 * D]
    gain_ffn = vector[2 * D : 3 * D]
    stream_low, pre_conv, mixed_low, pre_ffn, hidden_low, branch = saved
    normed_branch, branch_back = jax.vjp(normalize, branch)
    grad_gain_ffn = jnp.sum(grad_out * normed_branch, axis=0)
    grad_branch = branch_back(grad_out * gain_ffn)[0].astype(BF)
    grad_outer = contract_rows(hidden_low, grad_branch)
    grad_hidden = contract_cols(grad_branch, outer_mat)
    _, gelu_back = jax.vjp(jax.nn.gelu, pre_ffn)
    grad_pre_ffn = gelu_back(grad_hidden)[0].astype(BF)
    grad_bias_ffn = jnp.sum(grad_pre_ffn.astype(F32), axis=0)
    grad_inner = contract_rows(mixed_low, grad_pre_ffn)
    grad_mixed = grad_out + contract_cols(grad_pre_ffn, inner_mat)
    normed_conv, conv_back = jax.vjp(conv_branch, pre_conv)
    grad_gain_conv = jnp.sum(grad_mixed * normed_conv, axis=0)
    grad_pre_conv = conv_back(grad_mixed * gain_conv)[0].astype(BF)
    grad_conv_bias = jnp.sum(grad_pre_conv.astype(F32), axis=0)
    grad_kernel = contract_rows(columns(stream_low, dilation), grad_pre_conv)
    grad_stream = grad_mixed + fold_back(contract_cols(grad_pre_conv, conv_mat), dilation)
    vector_grad = jnp.concatenate([grad_conv_bias, grad_gain_conv, grad_gain_ffn, grad_bias_ffn])
    return (grad_stream, (grad_kernel, grad_inner, grad_outer, vector_grad))


def place():
    across = lax.axis_index("dp")
    index = lax.axis_index("fsdp")
    return across, index // (2 * NY), (index // 2) % NY, index % 2


def device(x, z, y, c):
    return (x, (z * NY + y) * 2 + c)


def shard(x, z, y, c):
    return x * (NZ * NY * 2) + (z * NY + y) * 2 + c


def meet(peers):
    barrier = pltpu.get_barrier_semaphore()
    for peer in peers:
        pl.semaphore_signal(barrier, inc=1, device_id=peer, device_id_type=MESH)
    pl.semaphore_wait(barrier, len(peers))


def neighbours(x, z, y, c):
    return [
        device(1 - x, z, y, c),
        device(x, z, 1 - y, c),
        device(x, z, y, 1 - c),
        device(x, (z + 1) % NZ, y, c),
        device(x, (z + 2) % NZ, y, c),
        device(x, (z + 3) % NZ, y, c),
    ]


def cut(rows, cols):
    if rows >= 32:
        first = (rows // 2 + 15) // 16 * 16
        return (0, first, 0, cols), (first, rows - first, 0, cols)
    if cols >= 256:
        return (0, rows, 0, cols // 2), (0, rows, cols // 2, cols // 2)
    return (0, rows, 0, cols), None


def gather_kernel(shapes, *refs):
    count = len(shapes)
    own_refs = refs[:count]
    full_refs = refs[count : 2 * count]
    own_sem, send_sem, recv_sem, half_sem = refs[2 * count :]
    x, z, y, c = place()
    meet(neighbours(x, z, y, c))
    to_x, to_y, to_c = device(1 - x, z, y, c), device(x, z, 1 - y, c), device(x, z, y, 1 - c)

    def rows_of(t, index, half=None):
        rows, cols = shapes[t]
        base = pl.multiple_of(index * rows, 16)
        if half is None:
            return full_refs[t].at[pl.ds(base, rows)]
        at, height, left, width = half
        base = pl.multiple_of(base + at, 16)
        if width == cols:
            return full_refs[t].at[pl.ds(base, height)]
        return full_refs[t].at[pl.ds(base, height), pl.ds(left, width)]

    def copy(t, index, kind, target, half=None, sem=None):
        part = rows_of(t, index, half)
        return pltpu.make_async_remote_copy(
            src_ref=part,
            dst_ref=part,
            send_sem=send_sem.at[t, kind],
            recv_sem=recv_sem.at[t, index] if sem is None else sem,
            device_id=target,
            device_id_type=MESH,
        )

    def arrive(t, index, half=None, sem=None):
        part = rows_of(t, index, half)
        pltpu.make_async_copy(part, part, recv_sem.at[t, index] if sem is None else sem).wait()

    def own(t):
        mine = shard(x, z, y, c)
        move = pltpu.make_async_copy(own_refs[t], rows_of(t, mine), own_sem.at[t])
        move.start()
        return move

    def along_z(t):
        mine = shard(x, z, y, c)
        for step in (1, 2, 3):
            copy(t, mine, 0, device(x, (z + step) % NZ, y, c)).start()
        spread(t, mine)

    def spread(t, index):
        copy(t, index, 1, to_x).start()
        copy(t, index, 2, to_y).start()
        copy(t, index, 3, to_c).start()

    def across(t):
        for step in (1, 2, 3):
            index = shard(x, (z + step) % NZ, y, c)
            arrive(t, index)
            spread(t, index)

    def corner(t):
        first, second = cut(*shapes[t])
        for step in range(NZ):
            level = (z + step) % NZ
            from_x = shard(1 - x, level, y, c)
            arrive(t, from_x)
            copy(t, from_x, 2, to_y, first).start()
            copy(t, from_x, 3, to_c).start()
            from_y = shard(x, level, 1 - y, c)
            arrive(t, from_y)
            if second is not None:
                copy(t, from_y, 1, to_x, second, half_sem.at[t, level]).start()
            copy(t, from_y, 3, to_c).start()

    def finish(t):
        first, second = cut(*shapes[t])
        for step in range(NZ):
            level = (z + step) % NZ
            far = shard(1 - x, level, 1 - y, c)
            arrive(t, far, first)
            if second is not None:
                arrive(t, far, second, half_sem.at[t, level])
            copy(t, far, 3, to_c).start()

    def settle(t):
        for ax in range(NX):
            for az in range(NZ):
                for ay in range(NY):
                    arrive(t, shard(ax, az, ay, 1 - c))

    def sent(t):
        rows, cols = shapes[t]
        first, second = cut(rows, cols)
        halves = [0 if half is None else half[1] * half[3] * NZ // cols for half in (second, first)]
        for kind, total in enumerate(
            (3 * rows, NZ * rows + halves[0], NZ * rows + halves[1], 16 * rows)
        ):
            part = full_refs[t].at[pl.ds(0, total)]
            pltpu.make_async_copy(part, part, send_sem.at[t, kind]).wait()

    moves = [own(t) for t in range(count)]
    moves[0].wait()
    along_z(0)
    for t in range(count):
        across(t)
        if t + 1 < count:
            moves[t + 1].wait()
            along_z(t + 1)
        corner(t)
        finish(t)
    for t in range(count):
        settle(t)
        sent(t)


def gather(shards):
    shapes = tuple(member.shape for member in shards)
    count = len(shapes)
    return pl.pallas_call(
        functools.partial(gather_kernel, shapes),
        out_shape=[jax.ShapeDtypeStruct((NDEV * r, w), BF) for r, w in shapes],
        in_specs=[pl.BlockSpec(memory_space=pl.ANY)] * count,
        out_specs=[pl.BlockSpec(memory_space=pl.ANY)] * count,
        scratch_shapes=[
            pltpu.SemaphoreType.DMA((count,)),
            pltpu.SemaphoreType.DMA((count, 4)),
            pltpu.SemaphoreType.DMA((count, NDEV)),
            pltpu.SemaphoreType.DMA((count, NZ)),
        ],
        compiler_params=pltpu.CompilerParams(collective_id=0, has_side_effects=True),
        name="gather",
    )(*shards)


def reduce_kernel(shapes, *refs):
    count = len(shapes)
    part_refs = refs[:count]
    out_refs = refs[count : 2 * count]
    scratch = refs[2 * count :]
    held, swap, first_in, second_in, from_x, from_y, total, from_z, result = (
        scratch[i * count : (i + 1) * count] for i in range(9)
    )
    local_sem, send_sem, recv_sem, out_sem = scratch[9 * count :]
    x, z, y, c = place()
    meet(neighbours(x, z, y, c))
    to_x, to_y, to_c = device(1 - x, z, y, c), device(x, z, 1 - y, c), device(x, z, y, 1 - c)

    def send(t, kind, src, dst, target):
        move = pltpu.make_async_remote_copy(
            src_ref=src,
            dst_ref=dst,
            send_sem=send_sem.at[t, kind],
            recv_sem=recv_sem.at[t, kind],
            device_id=target,
            device_id_type=MESH,
        )
        move.start()
        moves.append(move)
        return move

    moves = []
    live = {}

    def half_of(ref, half):
        at, height, left, width = half
        return ref.at[:, pl.ds(at, height), pl.ds(left, width)]

    def begin(t):
        live[t, "own"] = pltpu.make_async_copy(part_refs[t].at[:, c], held[t], local_sem.at[t])
        live[t, "own"].start()
        live[t, 0] = send(t, 0, part_refs[t].at[:, 1 - c], swap[t], to_c)

    def column(t, ax, ay):
        rows, cols = shapes[t]
        return held[t].reshape(NX, NZ, NY, rows, cols).at[ax, :, ay]

    def pair(t):
        live[t, "own"].wait()
        live[t, 0].wait_recv()

        @pl.loop(0, 16)
        def _(i):
            held[t][i] = (held[t][i].astype(F32) + swap[t][i].astype(F32)).astype(BF)

        first, second = cut(*shapes[t])
        far = column(t, 1 - x, 1 - y)
        live[t, 1] = send(t, 1, half_of(far, first), first_in[t], to_x)
        if second is not None:
            live[t, 2] = send(t, 2, half_of(far, second), second_in[t], to_y)
            live[t, 4] = send(
                t, 4, half_of(column(t, x, 1 - y), second), half_of(from_y[t], second), to_y
            )
        live[t, 3] = send(
            t, 3, half_of(column(t, 1 - x, y), first), half_of(from_x[t], first), to_x
        )

    def corner(t):
        first, second = cut(*shapes[t])
        rows, cols = shapes[t]
        live[t, 1].wait_recv()
        at, height, left, width = first

        @pl.loop(0, NZ)
        def _(i):
            j = (x * NZ + i) * NY + 1 - y
            spot = (j, pl.ds(at, height), pl.ds(left, width))
            held[t][spot] = (held[t][spot].astype(F32) + first_in[t][i].astype(F32)).astype(BF)

        live[t, 5] = send(
            t, 5, half_of(column(t, x, 1 - y), first), half_of(from_y[t], first), to_y
        )
        if second is not None:
            live[t, 2].wait_recv()
            low, tall, off, wide = second

            @pl.loop(0, NZ)
            def _(i):
                j = ((1 - x) * NZ + i) * NY + y
                spot = (j, pl.ds(low, tall), pl.ds(off, wide))
                held[t][spot] = (
                    held[t][spot].astype(F32) + second_in[t][i].astype(F32)
                ).astype(BF)

            live[t, 6] = send(
                t, 6, half_of(column(t, 1 - x, y), second), half_of(from_x[t], second), to_x
            )

    def line(t):
        for kind in (3, 4, 5, 6):
            if (t, kind) in live:
                live[t, kind].wait_recv()

        def summed(i):
            j = (x * NZ + i) * NY + y
            return (
                held[t][j].astype(F32) + from_x[t][i].astype(F32) + from_y[t][i].astype(F32)
            )

        for step in (1, 2, 3):
            level = (z + step) % NZ
            total[t][step - 1] = summed(level).astype(BF)
            live[t, 6 + step] = send(
                t, 6 + step, total[t].at[step - 1], from_z[t].at[step - 1], device(x, level, y, c)
            )
        result[t][...] = summed(z)

    def end(t):
        for step in (1, 2, 3):
            live[t, 6 + step].wait_recv()
        acc = result[t][...]
        for step in range(3):
            acc = acc + from_z[t][step].astype(F32)
        result[t][...] = acc
        live[t, "out"] = pltpu.make_async_copy(result[t], out_refs[t], out_sem.at[t])
        live[t, "out"].start()

    stages = (begin, pair, corner, line, end)
    for tick in range(count + len(stages) - 1):
        for lag, stage in enumerate(stages):
            if 0 <= tick - lag < count:
                stage(tick - lag)
    for move in moves:
        move.wait_send()
    for t in range(count):
        live[t, "out"].wait()


def reduce_shards(parts, shapes):
    count = len(shapes)

    def halves(which, dtype=BF):
        spaces = []
        for rows, cols in shapes:
            half = cut(rows, cols)[which]
            half = (0, 16, 0, 128) if half is None else half
            spaces.append(pltpu.VMEM((NZ, half[1], half[3]), dtype))
        return spaces

    def space(lead, dtype=BF):
        return [pltpu.VMEM(lead + shape, dtype) for shape in shapes]

    return pl.pallas_call(
        functools.partial(reduce_kernel, shapes),
        out_shape=[jax.ShapeDtypeStruct(shape, F32) for shape in shapes],
        in_specs=[pl.BlockSpec(memory_space=pl.ANY)] * count,
        out_specs=[pl.BlockSpec(memory_space=pl.ANY)] * count,
        scratch_shapes=[
            *space((16,)),
            *space((16,)),
            *halves(0),
            *halves(1),
            *space((NZ,)),
            *space((NZ,)),
            *space((3,)),
            *space((3,)),
            *space((), F32),
            pltpu.SemaphoreType.DMA((count,)),
            pltpu.SemaphoreType.DMA((count, 10)),
            pltpu.SemaphoreType.DMA((count, 10)),
            pltpu.SemaphoreType.DMA((count,)),
        ],
        compiler_params=pltpu.CompilerParams(
            collective_id=1, has_side_effects=True, vmem_limit_bytes=60 * 2**20
        ),
        name="reduce",
    )(*parts)


def gather_all(conv_weight, inner_weight, outer_weight, vectors):
    width = vectors.shape[1]
    padded = jnp.pad(vectors, ((0, 14), (0, 128 - width)))
    shards = []
    for b in range(2):
        shards += [
            conv_weight[b].reshape(-1, D),
            inner_weight[b].reshape(-1, FF),
            outer_weight[b].reshape(-1, D),
        ]
    full = gather([padded] + shards)
    flat = full[0].reshape(NDEV, 16, 128)[:, :2, :width]
    flat = flat.transpose(1, 0, 2).reshape(2, NV).astype(F32)
    return [tuple(full[1 + 3 * b : 4 + 3 * b]) + (flat[b],) for b in range(2)]


def reduce_all(grads, width):
    members, shapes = [], []
    for b in (1, 0):
        conv, inner, outer, _ = grads[b]
        for member in (outer, inner, conv):
            rows, cols = member.shape[0] // NDEV, member.shape[1]
            members.append(member.astype(BF).reshape(16, 2, rows, cols))
            shapes.append((rows, cols))
    vector = jnp.stack([grads[0][3], grads[1][3]]).reshape(2, NDEV, width).transpose(1, 0, 2)
    vector = jnp.pad(vector, ((0, 0), (0, 14), (0, 128 - width))).astype(BF)
    members.append(vector.reshape(16, 2, 16, 128))
    shapes.append((16, 128))
    outer1, inner1, conv1, outer0, inner0, conv0, vec = reduce_shards(members, tuple(shapes))

    def both(first, second):
        return jnp.stack([first.reshape(-1), second.reshape(-1)])

    return both(conv0, conv1), both(inner0, inner1), both(outer0, outer1), vec[:2, :width]


def gather_any(conv_weight, inner_weight, outer_weight, vectors):
    def whole(member):
        return lax.all_gather(member, ("dp", "fsdp"), axis=1, tiled=True)

    conv, inner, outer, vector = (
        whole(member) for member in (conv_weight, inner_weight, outer_weight, vectors)
    )
    return [
        (
            conv[b].reshape(KS * D, D),
            inner[b].reshape(D, FF),
            outer[b].reshape(FF, D),
            vector[b].astype(F32),
        )
        for b in range(2)
    ]


def reduce_any(grads, width):
    count_dp = lax.axis_size("dp")
    count_fsdp = lax.axis_size("fsdp")

    def settle(first, second):
        member = jnp.stack([first.reshape(-1), second.reshape(-1)]).astype(BF)
        member = member.reshape(2, count_dp, count_fsdp, -1)
        spread = lax.all_to_all(member, "fsdp", split_axis=2, concat_axis=2, tiled=True)
        partial = jnp.sum(spread.astype(F32), axis=2, keepdims=True).astype(BF)
        settled = lax.all_to_all(partial, "dp", split_axis=1, concat_axis=1, tiled=True)
        return jnp.sum(settled.astype(F32), axis=(1, 2))

    return tuple(settle(first, second) for first, second in zip(*grads))


def body(fast, embeddings, conv_weight, inner_weight, outer_weight, vectors, cotangent, row_mask):
    collect = gather_all if fast else gather_any
    weights = collect(conv_weight, inner_weight, outer_weight, vectors)
    stream = embeddings.astype(F32)
    saved = []
    for b in range(2):
        stream, kept = block_forward(stream, weights[b], DILATIONS[b])
        saved.append(kept)
    output = stream.astype(BF)
    grad_stream = cotangent.astype(F32) * row_mask.astype(F32)[:, None]
    grads = [None, None]
    for b in (1, 0):
        grad_stream, grads[b] = block_backward(grad_stream, saved[b], weights[b], DILATIONS[b])
    settle = reduce_all if fast else reduce_any
    conv, inner, outer, vector = settle(grads, vectors.shape[1])
    return output, grad_stream.astype(BF), conv, inner, outer, vector


def solution(mesh):
    rows = P(("dp", "fsdp"), None)
    flat = P(None, ("dp", "fsdp"))
    fast = mesh.shape["dp"] == NX and mesh.shape["fsdp"] == NZ * NY * 2
    return jax.shard_map(
        functools.partial(body, fast),
        mesh=mesh,
        in_specs=(rows, flat, flat, flat, flat, rows, P(("dp", "fsdp"))),
        out_specs=(rows, rows, flat, flat, flat, flat),
        check_vma=False,
    )
```

time: 1220 us -> 516 us (0.42)
  other arithmetic: 481 us -> 68.3 us
  waiting for transfers between devices: 361 us -> 0 us
  Pallas kernels: 0 us -> 203 us
  blocking collectives: 42.2 us -> 0 us
  local copies, waits for them, and re-layouts: 155 us -> 117 us
  starting transfers between devices: 36.5 us -> 0 us
  between operations: 16.3 us -> 1.71 us
    all_gather x6 -> x0, other arithmetic: 381 us -> none  [the longest x2 202 us: body(): lax.all_gather(conv_weight[block_id], ('dp', 'fsdp'), axis=0, tiled=True)]
    all_to_all x8 -> x0, waiting for transfers between devices: 267 us -> none  [the longest x4 260 us: reduce_both(): lax.all_to_all(shortened(shaped), 'fsdp', split_axis=2, concat_axis=2, ti...]
    pallas_call x0 -> x2, Pallas kernels: none -> 203 us  [the longest x1 105 us: gather(): pl.pallas_call(functools.partial(gather_kernel, shapes), out_shape=[jax.S...]
    all_gather x6 -> x0, waiting for transfers between devices: 91.8 us -> none  [the longest x2 36.9 us: body(): lax.all_gather(conv_weight[block_id], ('dp', 'fsdp'), axis=0, tiled=True)]
    add x14 -> x0, local copies, waits for them, and re-layouts: 61.2 us -> none  [body(): total + update]
    unnamed x1 -> x0, blocking collectives: 42.2 us -> none
    all_to_all x8 -> x0, starting transfers between devices: 36.3 us -> none  [the longest x4 22.5 us: reduce_both(): lax.all_to_all(shortened(shaped), 'fsdp', split_axis=2, concat_axis=2, ti...]
    reduce_sum x13 -> x2, other arithmetic: 34.9 us -> 4.14 us  [block_backward(): grad_conv_bias = jnp.sum(grad_pre_conv.astype(F32), axis=0)]
  transfers between devices with their start and end apart: 14 -> 0, of which waited for: 9 -> 0; matrix products, arithmetic and copies ran while one was open for 42% -> 0% of each run, Pallas kernels for 0% -> 0%
where the time goes in v1:
time: 516 us; the launch traced here: 508 us
  Pallas kernels  203 us (39%)
  matrix products  119 us (23%)
  local copies, waits for them, and re-layouts  117 us (23%)
  other arithmetic  68.3 us (13%)
    pallas_call x1, Pallas kernels, gather(): pl.pallas_call(functools.partial(gather_kernel, shapes), out_shape=[jax.S...  105 us
    pallas_call x1, Pallas kernels, reduce_shards(): pl.pallas_call(functools.partial(reduce_kernel, shapes), out_shape=[jax.S...  98.6 us
    dot_general x6, matrix products, contract_cols(): lax.dot_general(left, right, (((1,), (1,)), ((), ())), preferred_element_...  49.9 us
    reshape x2, local copies, waits for them, and re-layouts, fold_back(): framed = grad_cols.reshape(windows, L, KS, D)  49.3 us
    add x4, other arithmetic, fold_back(): total + jnp.pad(framed[:, :, tap_id], ((0, 0), (before, 2 * margin - befo...  39.9 us
    dot_general x6, matrix products, contract_rows(): lax.dot_general(left, right, (((0,), (0,)), ((), ())), preferred_element_...  33.9 us
    squeeze x2, local copies, waits for them, and re-layouts, fold_back(): framed[:, :, tap_id]  21.5 us
    unnamed x111, local copies, waits for them, and re-layouts  17.5 us

profile of v1, /device:TPU:12, one launch (start us, length us, event | category | flops | bytes accessed | tf_op | source)
XLA Modules:
  0.0 508.5 jit_solution(3289451909452112200)
XLA Ops:
  2.7 1.7 slice_reduce_fusion.3
  5.7 1.7 slice_reduce_fusion.2
  8.8 2.7 slice_reduce_fusion
  13.0 1.6 pad_slice_fusion.8
  24.4 104.6 %gather.1 = (bf16[512,128]{1,0:T(8,128)(2,1)}, bf16[4608,512]{1,0:T(8,128)(2,1)}, bf16[512,2048]{1,0:T(8,128)(2,1)}, bf16[2048,512]{1,0:T(8,128)(2,1)}, bf16[460...) custom-call(bf16[16,128]{1,0:T(8,128)(2,1)} %pad.91.refs_0_, ...), custom_call_target="tpu_custom_call" | custom-call | tf_op jit(solution)/shard_map/gather/pallas_call | solution.py:265
  130.1 9.7 %fusion.40 = (f32[1024]{0:T(1024)S(1)}, f32[1024,512]{1,0:T(8,128)S(1)}) fusion(f32[512]{0:T(512)S(1)} %bitcast.170, bf16[1024,4608]{1,0:T(8,128)(2,1)} %constant_dynamic-update-slice_fusion, bf16[4608,512]{1,0:T(8,128)(2,1)} %get-tuple-element.21), kind=kOutput, calls=%fused_computation.179 | convolution fusion | flops 4837080064 | bytes 16259072 | tf_op jit(solution)/shard_map/dot_general | solution.py:72
  140.9 1.3 copy-done.27
  142.1 7.2 %multiply_convert_fusion.1 = (bf16[1024,2048]{1,0:T(8,128)(2,1)S(1)}, f32[1024,2048]{1,0:T(8,128)}) fusion(f32[2048]{0:T(1024)S(1)} %bitcast.197, bf16[512,2048]{1,0:T(8,128)(2,1)S(1)} %copy-done.27, bf16[1024,512]{1,0:T(8,128)(2,1)S(1)} %copy-done.5, f32[1024]{0:T(1024)S(1)} %fusion.35, f32[1024]{0:T(1024)S(1)} %broadcast_multiply_fusion.3, ...), kind=kOutput, calls=%fused_computation.19 | convolution fusion | flops 2176319488 | bytes 17846272 | tf_op jit(solution)/shard_map/dot_general | solution.py:76
  149.3 2.4 fusion.55
  152.3 1.8 fusion.52
  155.6 1.6 slice-done.3
  157.4 5.6 %fusion.39 = (f32[1024]{0:T(1024)S(1)}, f32[1024,512]{1,0:T(8,128)S(1)}) fusion(f32[512]{0:T(512)S(1)} %bitcast.178, bf16[1024,4608]{1,0:T(8,128)(2,1)S(1)} %constant_dynamic-update-slice_fusion.9, bf16[4608,512]{1,0:T(8,128)(2,1)S(1)} %bitcast.203), kind=kOutput, calls=%fused_computation.178 | convolution fusion | flops 4837080064 | bytes 16259072 | tf_op jit(solution)/shard_map/dot_general | solution.py:72
  165.7 6.3 %multiply_convert_fusion = (bf16[1024,2048]{1,0:T(8,128)(2,1)S(1)}, f32[1024,2048]{1,0:T(8,128)}) fusion(f32[2048]{0:T(1024)S(1)} %bitcast.199, bf16[512,2048]{1,0:T(8,128)(2,1)S(1)} %copy-done.31, f32[1024,512]{1,0:T(8,128)S(1)} %multiply_add_fusion), kind=kOutput, calls=%fused_computation.18 | convolution fusion | flops 2168979456 | bytes 16785408 | tf_op jit(solution)/shard_map/dot_general | solution.py:76
  171.9 3.8 fusion.56
  175.8 3.0 copy.36
  178.8 2.1 multiply_reduce_fusion.8
  182.5 2.0 fusion.51
  184.6 10.2 %fusion.57 = (bf16[2048]{0:T(1024)(128)(2,1)S(1)}, bf16[1024,2048]{1,0:T(8,128)(2,1)S(1)}) fusion(f32[1024,2048]{1,0:T(8,128)} %get-tuple-element.115, f32[2048]{0:T(1024)S(1)} %bitcast.200, bf16[2048,512]{1,0:T(8,128)(2,1)S(1)} %copy-done.34, f32[1024,512]{1,0:T(8,128)S(1)} %get-tuple-element.60, f32[1024]{0:T(1024)S(1)} %negate_multiply_fusion.3), kind=kOutput, calls=%fused_computation.192 | convolution fusion | flops 2194667520 | bytes 16793600 | tf_op jit(solution)/shard_map/dot_general | solution.py:37
  194.8 3.9 convolution_convert_fusion.5
  198.7 3.9 convolution_convert_fusion.4
  202.6 3.3 multiply_reduce_fusion.1
  205.9 1.6 fusion.50
  207.5 2.1 fusion.46
  209.7 7.1 %convolution_convert_fusion.1 = bf16[4608,512]{1,0:T(8,128)(2,1)} fusion(bf16[1024,4608]{1,0:T(8,128)(2,1)S(1)} %bitcast.169, bf16[1024,512]{1,0:T(8,128)(2,1)S(1)} %get-tuple-element.51), kind=kOutput, calls=%fused_computation.21 | convolution fusion | flops 4834197504 | bytes 15204352 | tf_op jit(solution)/shard_map/dot_general | solution.py:33
  216.8 11.5 %fusion.59 = f32[1024,4608]{0,1:T(8,128)} fusion(bf16[1024,512]{1,0:T(8,128)(2,1)S(1)} %get-tuple-element.51, bf16[4608,512]{1,0:T(8,128)(2,1)} %get-tuple-element.24), kind=kOutput, calls=%fused_computation.194 | convolution fusion | flops 4831838208 | bytes 24641536 | tf_op jit(solution)/shard_map/dot_general | solution.py:37
  228.3 24.6 %reshape.206 = f32[2,512,9,512]{1,0,3,2:T(2,128)} reshape(f32[1024,4608]{0,1:T(8,128)} %fusion.59) | data formatting | bytes 37748736 | tf_op jit(solution)/shard_map/reshape | solution.py:53
  252.9 10.6 %slice_bitcast_fusion.17 = (f32[2,512,512]{1,0,2:T(2,128)S(1)}, f32[2,512,512]{1,0,2:T(2,128)S(1)}, f32[2,512,512]{1,0,2:T(2,128)S(1)}, f32[2,512,512]{1,0,2:T(2...) fusion(f32[2,512,9,512]{1,0,3,2:T(2,128)} %reshape.206), kind=kLoop, calls=%fused_computation.79 | loop fusion | bytes 37748736 | tf_op jit(solution)/shard_map/squeeze | solution.py:59
  263.6 5.7 %pad_add_fusion.1 = f32[2,640,512]{1,0,2:T(2,128)S(1)} fusion(f32[2,512,512]{1,0,2:T(2,128)S(1)} %get-tuple-element.79, f32[2,512,512]{1,0,2:T(2,128)S(1)} %get-tuple-element.80, f32[2,512,512]{1,0,2:T(2,128)S(1)} %get-tuple-element.72), kind=kLoop, calls=%fused_computation.35 | loop fusion | flops 1310720 | bytes 8912896 | tf_op jit(solution)/shard_map/add | solution.py:58
  269.3 14.4 %pad_add_fusion.8 = f32[2,512,512]{1,0,2:T(2,128)} fusion(f32[2,512,512]{1,0,2:T(2,128)S(1)} %get-tuple-element.73, f32[2,512,512]{1,0,2:T(2,128)S(1)} %get-tuple-element.74, f32[2,512,512]{1,0,2:T(2,128)S(1)} %get-tuple-element.75, f32[2,512,512]{1,0,2:T(2,128)S(1)} %get-tuple-element.76, f32[2,512,512]{1,0,2:T(2,128)S(1)} %get-tuple-element.77, ...), kind=kLoop, calls=%fused_computation.65 | loop fusion | flops 3145728 | bytes 16777216 | tf_op jit(solution)/shard_map/add | solution.py:58
  283.6 4.3 copy.39
  287.9 3.1 multiply_reduce_fusion.2
  292.7 10.1 %fusion.58 = (bf16[2048]{0:T(1024)(128)(2,1)S(1)}, bf16[1024,2048]{1,0:T(8,128)(2,1)S(1)}) fusion(f32[1024,2048]{1,0:T(8,128)} %get-tuple-element.109, f32[2048]{0:T(1024)S(1)} %bitcast.198, bf16[2048,512]{1,0:T(8,128)(2,1)S(1)} %copy-done.30, f32[1024,512]{1,0:T(8,128)S(1)} %get-tuple-element.55, f32[1024]{0:T(1024)S(1)} %negate_multiply_fusion.1), kind=kOutput, calls=%fused_computation.193 | convolution fusion | flops 2194667520 | bytes 16793600 | tf_op jit(solution)/shard_map/dot_general | solution.py:37
  302.9 3.9 convolution_convert_fusion.3
  306.8 3.3 multiply_reduce_fusion.3
  310.2 4.5 convolution_convert_fusion.2
  314.7 1.6 fusion.48
  316.3 2.1 fusion.44
  318.4 10.7 %convolution_convert_fusion = bf16[4608,512]{1,0:T(8,128)(2,1)} fusion(bf16[1024,4608]{1,0:T(8,128)(2,1)} %constant_dynamic-update-slice_fusion, bf16[1024,512]{1,0:T(8,128)(2,1)S(1)} %get-tuple-element.49), kind=kOutput, calls=%fused_computation.20 | convolution fusion | flops 4834197504 | bytes 15204352 | tf_op jit(solution)/shard_map/dot_general | solution.py:33
  330.0 98.6 %reduce.21 = (f32[64,512]{1,0:T(8,128)}, f32[16,2048]{1,0:T(8,128)}, f32[144,512]{1,0:T(8,128)}, f32[64,512]{1,0:T(8,128)}, f32[16,2048]{1,0:T(8,128)}, /*index=5*/f32[144,512]{1,0:T(8,128)}, f32[16,128]{1,0:T(8,128)}) custom-call(bf16[16,2,64,512]{3,2,1,0:T(8,128)(2,1)} %bitcast.151, bf16[16,2,16,2048]{3,2,1,0:T(8,128)(2,1)} %bitcast.152, ...), custom_call_target="tpu_custom_call" | custom-call | tf_op jit(solution)/shard_map/reduce/pallas_call | solution.py:428
  428.6 1.3 copy.49
  431.2 1.3 pad_maximum_fusion
  435.7 11.4 %fusion.60 = f32[1024,4608]{0,1:T(8,128)} fusion(bf16[1024,512]{1,0:T(8,128)(2,1)S(1)} %get-tuple-element.49, bf16[4608,512]{1,0:T(8,128)(2,1)} %get-tuple-element.21), kind=kOutput, calls=%fused_computation.195 | convolution fusion | flops 4831838208 | bytes 24641536 | tf_op jit(solution)/shard_map/dot_general | solution.py:37
  447.1 24.6 %reshape.208 = f32[2,512,9,512]{1,0,3,2:T(2,128)} reshape(f32[1024,4608]{0,1:T(8,128)} %fusion.60) | data formatting | bytes 37748736 | tf_op jit(solution)/shard_map/reshape | solution.py:53
  471.8 10.8 %slice_bitcast_fusion.8 = (f32[2,512,512]{1,0,2:T(2,128)S(1)}, f32[2,512,512]{1,0,2:T(2,128)S(1)}, f32[2,512,512]{1,0,2:T(2,128)S(1)}, f32[2,512,512]{1,0,2:T(2,...) fusion(f32[2,512,9,512]{1,0,3,2:T(2,128)} %reshape.208), kind=kLoop, calls=%fused_computation.64 | loop fusion | bytes 37748736 | tf_op jit(solution)/shard_map/squeeze | solution.py:59
  482.6 5.7 %pad_add_fusion = f32[2,528,512]{1,0,2:T(2,128)S(1)} fusion(f32[2,512,512]{1,0,2:T(2,128)S(1)} %get-tuple-element.70, f32[2,512,512]{1,0,2:T(2,128)S(1)} %get-tuple-element.71, f32[2,512,512]{1,0,2:T(2,128)S(1)} %get-tuple-element.63), kind=kLoop, calls=%fused_computation.34 | loop fusion | flops 1081344 | bytes 8454144 | tf_op jit(solution)/shard_map/add | solution.py:58
  488.3 14.2 %pad_add_fusion.2 = f32[2,512,512]{1,0,2:T(2,128)} fusion(f32[2,512,512]{1,0,2:T(2,128)S(1)} %get-tuple-element.64, f32[2,512,512]{1,0,2:T(2,128)S(1)} %get-tuple-element.65, f32[2,512,512]{1,0,2:T(2,128)S(1)} %get-tuple-element.66, f32[2,512,512]{1,0,2:T(2,128)S(1)} %get-tuple-element.67, f32[2,512,512]{1,0,2:T(2,128)S(1)} %get-tuple-element.68, ...), kind=kLoop, calls=%fused_computation.50 | loop fusion | flops 3145728 | bytes 16777216 | tf_op jit(solution)/shard_map/add | solution.py:58
  502.5 2.7 copy.41
  505.2 3.0 fusion.28
  (156 shorter events, 31.4 us)
Async XLA Ops:
  0.6 12.4 %copy-start.5 = (bf16[1024,512]{1,0:T(8,128)(2,1)S(1)}, bf16[1024,512]{1,0:T(8,128)(2,1)}, u32[]{:S(2)}) copy-start(bf16[1024,512]{1,0:T(8,128)(2,1)} %param.7) | copy-start | bytes 3145732
  130.1 22.2 %copy-start.19 = (f32[1,512]{1,0:T(1,128)}, f32[1,512]{1,0:T(1,128)S(1)}, u32[]{:S(2)}) copy-start(f32[1,512]{1,0:T(1,128)S(1)} %get-tuple-element.102) | copy-start | bytes 6148
  130.1 22.2 %copy-start.25 = (f32[1,512]{1,0:T(1,128)}, f32[1,512]{1,0:T(1,128)S(1)}, u32[]{:S(2)}) copy-start(f32[1,512]{1,0:T(1,128)S(1)} %get-tuple-element.103) | copy-start | bytes 6148
  139.8 12.5 %copy-start.1 = (f32[1024,512]{1,0:T(8,128)}, f32[1024,512]{1,0:T(8,128)S(1)}, u32[]{:S(2)}) copy-start(f32[1024,512]{1,0:T(8,128)S(1)} %get-tuple-element.107) | copy-start | bytes 6291460
  139.8 2.4 copy-start.27
  139.8 12.4 %copy-start.17 = (f32[1024]{0:T(1024)}, f32[1024]{0:T(1024)S(1)}, u32[]{:S(2)}) copy-start(f32[1024]{0:T(1024)S(1)} %broadcast_multiply_fusion.3) | copy-start | bytes 12292
  140.8 8.5 %copy-start.21 = (f32[1024]{0:T(1024)}, f32[1024]{0:T(1024)S(1)}, u32[]{:S(2)}) copy-start(f32[1024]{0:T(1024)S(1)} %multiply_reduce_fusion.11) | copy-start | bytes 12292
  142.1 10.1 %copy-start.23 = (f32[1024]{0:T(1024)}, f32[1024]{0:T(1024)S(1)}, u32[]{:S(2)}) copy-start(f32[1024]{0:T(1024)S(1)} %fusion.35) | copy-start | bytes 12292
  142.1 7.2 %copy-start.29 = (bf16[2048,512]{1,0:T(8,128)(2,1)S(1)}, bf16[2048,512]{1,0:T(8,128)(2,1)}, u32[]{:S(2)}) copy-start(bf16[2048,512]{1,0:T(8,128)(2,1)} %get-tuple-element.23) | copy-start | bytes 6291460
  149.3 2.4 copy-start.35
  151.8 2.3 copy-start.3
  155.1 2.2 slice-start.3
  155.3 2.1 slice-start.4
  157.4 5.6 %copy-start.16 = (bf16[1024,4608]{1,0:T(8,128)(2,1)}, bf16[1024,4608]{1,0:T(8,128)(2,1)S(1)}, u32[]{:S(2)}) copy-start(bf16[1024,4608]{1,0:T(8,128)(2,1)S(1)} %constant_dynamic-update-slice_fusion.9) | copy-start | bytes 28311556
  164.1 1.6 copy-start.31
  165.7 6.3 %copy-start.8 = (f32[1024,512]{1,0:T(8,128)}, f32[1024,512]{1,0:T(8,128)S(1)}, u32[]{:S(2)}) copy-start(f32[1024,512]{1,0:T(8,128)S(1)} %multiply_add_fusion) | copy-start | bytes 6291460
  165.7 6.3 %copy-start.33 = (bf16[2048,512]{1,0:T(8,128)(2,1)S(1)}, bf16[2048,512]{1,0:T(8,128)(2,1)}, u32[]{:S(2)}) copy-start(bf16[2048,512]{1,0:T(8,128)(2,1)} %get-tuple-element.26) | copy-start | bytes 6291460
  171.9 3.8 copy-start.37
  175.8 5.2 %copy-start.11 = (bf16[1024,512]{1,0:T(8,128)(2,1)S(1)}, bf16[1024,512]{1,0:T(8,128)(2,1)}, u32[]{:S(2)}) copy-start(bf16[1024,512]{1,0:T(8,128)(2,1)} %param.12) | copy-start | bytes 3145732
  178.8 2.2 copy-start
  180.9 1.6 copy-start.9
  182.5 2.0 copy-start.34
  184.6 10.2 %copy-start.38 = (bf16[1024,2048]{1,0:T(8,128)(2,1)S(1)}, bf16[1024,2048]{1,0:T(8,128)(2,1)}, u32[]{:S(2)}) copy-start(bf16[1024,2048]{1,0:T(8,128)(2,1)} %copy-done.37) | copy-start | bytes 12582916
  198.7 3.9 copy-start.32
  198.7 10.9 %slice-start = ((s8[9437184]{0:T(1024)(128)(4,1)}), s8[4194304]{0:T(1024)(128)(4,1)S(1)}, s32[]{:S(2)}) async-start(s8[9437184]{0:T(1024)(128)(4,1)} %bitcast.168), calls=%async_computation | async-start | bytes 8388608
  202.6 7.1 %slice-start.1 = ((s8[9437184]{0:T(1024)(128)(4,1)}), s8[4194304]{0:T(1024)(128)(4,1)S(1)}, s32[]{:S(2)}) async-start(s8[9437184]{0:T(1024)(128)(4,1)} %bitcast.168), calls=%async_computation.1 | async-start | bytes 8388608
  202.6 7.1 %slice-start.2 = ((s8[9437184]{0:T(1024)(128)(4,1)}), s8[1048576]{0:T(1024)(128)(4,1)S(1)}, s32[]{:S(2)}) async-start(s8[9437184]{0:T(1024)(128)(4,1)} %bitcast.168), calls=%async_computation.2 | async-start | bytes 2097152
  205.9 1.7 copy-start.10
  283.6 4.3 copy-start.4
  291.1 1.6 copy-start.30
  292.7 10.1 %copy-start.36 = (bf16[1024,2048]{1,0:T(8,128)(2,1)S(1)}, bf16[1024,2048]{1,0:T(8,128)(2,1)}, u32[]{:S(2)}) copy-start(bf16[1024,2048]{1,0:T(8,128)(2,1)} %copy-done.35) | copy-start | bytes 12582916
  302.8 3.9 copy-start.2
  302.8 3.9 copy-start.18
  302.8 3.9 copy-start.20
  302.9 3.9 copy-start.24
  302.9 3.9 copy-start.26
  302.9 3.9 copy-start.28
  306.8 3.4 copy-start.22
  306.8 3.4 copy-start.6
  310.1 4.6 copy-start.7
  428.6 5.2 %copy-start.15 = (f32[16,2048]{1,0:T(8,128)S(1)}, f32[16,2048]{1,0:T(8,128)}, u32[]{:S(2)}) copy-start(f32[16,2048]{1,0:T(8,128)} %get-tuple-element.29) | copy-start | bytes 393220
  428.6 5.4 %copy-start.14 = (f32[16,2048]{1,0:T(8,128)S(1)}, f32[16,2048]{1,0:T(8,128)}, u32[]{:S(2)}) copy-start(f32[16,2048]{1,0:T(8,128)} %get-tuple-element.30) | copy-start | bytes 393220
  428.6 5.5 %copy-start.13 = (f32[64,512]{1,0:T(8,128)S(1)}, f32[64,512]{1,0:T(8,128)}, u32[]{:S(2)}) copy-start(f32[64,512]{1,0:T(8,128)} %get-tuple-element.31) | copy-start | bytes 393220
  428.6 5.7 %copy-start.12 = (f32[64,512]{1,0:T(8,128)S(1)}, f32[64,512]{1,0:T(8,128)}, u32[]{:S(2)}) copy-start(f32[64,512]{1,0:T(8,128)} %get-tuple-element.32) | copy-start | bytes 393220
